TPU v7x, 1024 devices: a whole 4x4x32 slice. The times are simulated.
1024 devices in a mesh: row: 16 (over z_lo), col: 8 (over y, core), layer: 8 (over z_hi, x).
Axes of the slice: x: 4, y: 4, z: 32 (z_hi: 2, z_lo: 16; z = z_hi * 16 + z_lo), core: 2. Of those that a mesh axis runs over, the one named last changes fastest.
Arguments:
- density: bfloat16 [6144, 6144], P('row', 'col'), may hold values from -0.5 to 0.5
- occupancy: int32 [48, 48], replicated, may hold values from 0 to 1, as said below
Outputs:
- purified: float32 [6144, 6144], P(('row', 'layer'), 'col')
Inputs may be any that keep to these rules, and one draw needn't show every extreme that they name: `occupancy`: block (i, j) is occupied wherever |i - j| <= 8; other blocks may or may not be.
All inputs are finite; a program needn't handle non-finite values.
Results may differ from a plain program's by a relative error of at most 0.0029.
Values may be sent and summed in bfloat16 or wider, within the bound.
A program may use at most 32 MiB of HBM per device.

v0:
```python
import jax
import jax.numpy as jnp
from jax import lax
from jax.sharding import PartitionSpec as P

BS = 128


def from_root(value, axis, source):
    kept = jnp.where(lax.axis_index(axis) == source, value, 0).astype(value.dtype)
    return lax.psum(kept, axis)


def spread(occupied, block_size):
    row_blocks, column_blocks = occupied.shape
    widened = jnp.broadcast_to(
        occupied[:, None, :, None], (row_blocks, block_size, column_blocks, block_size)
    )
    return widened.reshape(row_blocks * block_size, column_blocks * block_size)


def shards(density, occupancy):
    row_count = lax.axis_size("row")
    column_count = lax.axis_size("col")
    layer_count = lax.axis_size("layer")
    row_index = lax.axis_index("row")
    column_index = lax.axis_index("col")
    layer_index = lax.axis_index("layer")
    tile_rows, tile_cols = density.shape
    occupied_tile = lax.dynamic_slice(
        occupancy,
        (row_index * (tile_rows // BS), column_index * (tile_cols // BS)),
        (tile_rows // BS, tile_cols // BS),
    )
    pattern = spread(occupied_tile.astype(jnp.bfloat16), BS)
    masked = density * pattern
    per_layer = column_count // layer_count
    per_column = row_count // column_count
    slab_rows = tile_rows // layer_count
    pattern_wide = pattern.astype(jnp.float32)
    slab_pattern = lax.dynamic_slice_in_dim(pattern_wide, layer_index * slab_rows, slab_rows, 0)

    def reduce_rows(partial_value):
        return lax.psum_scatter(partial_value, "layer", scatter_dimension=0, tiled=True)

    leading = layer_index * per_layer
    panels = [from_root(masked, "col", leading + 0)]

    def stacked_rows(source, owner_tile):
        return jnp.concatenate(
            [
                from_root(source, "row", owner_tile * per_column + within)
                for within in range(per_column)
            ],
            axis=0,
        )

    def product(source):
        running = jnp.dot(
            panels[0], stacked_rows(source, leading + 0), preferred_element_type=jnp.float32
        )
        return running

    square_slab = (reduce_rows(product(masked)) * slab_pattern).astype(jnp.bfloat16)
    square_tile = lax.all_gather(square_slab, "layer", axis=0, tiled=True)
    cube_slab = reduce_rows(product(square_tile)) * slab_pattern
    return 3.0 * square_slab.astype(jnp.float32) - 2.0 * cube_slab


def solution(mesh):
    return jax.shard_map(
        shards,
        mesh=mesh,
        in_specs=(P("row", "col"), P()),
        out_specs=P(("row", "layer"), "col"),
        check_vma=False,
    )
```

profile of v0, /device:TPU:1, one launch (start us, length us, event | category | flops | bytes accessed | tf_op | source)
XLA Modules:
  0.0 1387.9 jit_solution(12948623736579937168)
XLA Ops:
  6.5 0.0 copy-start
  6.5 0.0 all-reduce.6.cloned.1.call-start
  6.5 0.8 dynamic-slice_convert_fusion
  7.4 0.2 broadcast_in_dim.14
  7.6 0.1 copy-done
  7.6 0.9 broadcast_select_fusion.3
  8.5 1.1 broadcast_select_fusion.1
  9.6 0.0 all-reduce.6.cloned.1.call-update
  9.7 0.0 all-reduce.10.cloned.1.call-start
  9.7 0.7 all-reduce.10.cloned.1.call-update
  10.4 0.0 reduce-scatter.3.cloned.1.call-start
  10.5 104.7 %all-reduce.6.cloned.1.call-done = bf16[384,768]{1,0:T(8,128)(2,1)} async-done(((bf16[384,768]{1,0:T(8,128)(2,1)}), bf16[384,768]{1,0:T(8,128)(2,1)}) %all-reduce.6.cloned.1.call-update) | async-done | bytes 589840 | tf_op jit(solution)/shard_map/psum | solution.py:11
  115.1 365.5 %all-reduce.10.cloned.1.call-done = (bf16[384,768]{1,0:T(8,128)(2,1)}, bf16[384,768]{1,0:T(8,128)(2,1)}) async-done(((bf16[384,768]{1,0:T(8,128)(2,1)}, bf16[384,768]{1,0:T(8,128)(2,1)}), (bf16[384,768]{1,0:T(8,128)(2,1)}, bf16[384,768]{1,0:T(8,128)(2,1)})) %all-reduce.10.cloned.1.call-update) | async-done | bytes 1179664 | tf_op jit(solution)/shard_map/psum | solution.py:11
  480.6 3.1 fusion
  483.7 0.0 reduce-scatter.3.cloned.1.call-update
  483.7 0.0 all-reduce.8.cloned.1.call-start
  483.8 217.4 %reduce-scatter.3.cloned.1.call-done = f32[48,768]{1,0:T(8,128)} async-done(((f32[384,768]{1,0:T(8,128)}), f32[48,768]{1,0:T(8,128)}) %reduce-scatter.3.cloned.1.call-update) | async-done | bytes 147472 | tf_op jit(solution)/shard_map/reduce_scatter | solution.py:44
  701.2 0.9 fusion.10
  702.2 98.7 %all_gather.3 = bf16[384,768]{1,0:T(8,128)(2,1)S(1)} all-gather(bf16[48,768]{1,0:T(8,128)(2,1)S(1)} %fusion.10), channel_id=1, replica_groups=mesh['row'=16,'col'=8,'layer'=8] {'layer'}, dimensions={0}, use_global_device_ids=true | all-gather | bytes 663552 | tf_op jit(solution)/shard_map/all_gather | solution.py:65
  800.8 0.0 copy-start.1
  800.8 1.1 broadcast_select_fusion.2
  802.0 0.0 all-reduce.8.cloned.1.call-update
  802.0 0.0 reduce-scatter.5.cloned.1.call-start
  802.0 356.4 %all-reduce.8.cloned.1.call-done = (bf16[384,768]{1,0:T(8,128)(2,1)}, bf16[384,768]{1,0:T(8,128)(2,1)}) async-done(((bf16[384,768]{1,0:T(8,128)(2,1)}, bf16[384,768]{1,0:T(8,128)(2,1)}), (bf16[384,768]{1,0:T(8,128)(2,1)}, bf16[384,768]{1,0:T(8,128)(2,1)})) %all-reduce.8.cloned.1.call-update) | async-done | bytes 1179664 | tf_op jit(solution)/shard_map/psum | solution.py:11
  1158.4 0.0 copy-done.1
  1158.4 2.9 fusion.4
  1161.3 0.0 reduce-scatter.5.cloned.1.call-update
  1161.3 218.4 %reduce-scatter.5.cloned.1.call-done = f32[48,768]{1,0:T(8,128)} async-done(((f32[384,768]{1,0:T(8,128)}), f32[48,768]{1,0:T(8,128)}) %reduce-scatter.5.cloned.1.call-update) | async-done | bytes 147472 | tf_op jit(solution)/shard_map/reduce_scatter | solution.py:44
  1379.8 1.6 fusion.9
Async XLA Ops:
  6.5 1.1 copy-start
  6.5 108.6 %all-reduce.6.cloned.1.call-start = ((), (), s32[]{:S(2)}) async-start(), calls=%async_computation.2 | async-start | bytes 1179648 | tf_op jit(solution)/shard_map/psum | solution.py:11
  9.7 471.0 %all-reduce.10.cloned.1.call-start = ((), (), s32[]{:S(2)}) async-start(), calls=%async_computation.6 | async-start | bytes 2359296 | tf_op jit(solution)/shard_map/psum | solution.py:11
  10.4 690.8 %reduce-scatter.3.cloned.1.call-start = ((), (), s32[]{:S(2)}) async-start(), calls=%async_computation.3 | async-start | bytes 1327104 | tf_op jit(solution)/shard_map/reduce_scatter | solution.py:44
  483.7 674.7 %all-reduce.8.cloned.1.call-start = ((), (), s32[]{:S(2)}) async-start(), calls=%async_computation.5 | async-start | bytes 2359296 | tf_op jit(solution)/shard_map/psum | solution.py:11
  800.8 357.6 %copy-start.1 = (bf16[384,768]{1,0:T(8,128)(2,1)S(1)}, bf16[384,768]{1,0:T(8,128)(2,1)}, u32[]{:S(2)}) copy-start(bf16[384,768]{1,0:T(8,128)(2,1)} %all-reduce.6.cloned.1.call-done) | copy-start | bytes 1769476
  802.0 577.8 %reduce-scatter.5.cloned.1.call-start = ((), (), s32[]{:S(2)}) async-start(), calls=%async_computation.4 | async-start | bytes 1327104 | tf_op jit(solution)/shard_map/reduce_scatter | solution.py:44
Sparse Core Ops, SparseCore 0:
  9.8 105.3 all-reduce.5
  118.7 361.8 all-reduce.9
  486.4 214.7 reduce-scatter.2
  802.1 356.2 all-reduce.7
  1165.0 214.7 reduce-scatter.4
where the time goes:
time: 1390 us
  waiting for transfers between devices  1260 us (91%)
  blocking collectives  98.7 us (7%)
    psum x3, waiting for transfers between devices, from_root(): return lax.psum(kept, axis)  827 us
    reduce_scatter x2, waiting for transfers between devices, reduce_rows(): lax.psum_scatter(partial_value, 'layer', scatter_dimension=0, tiled=True)  436 us
    all_gather x1, blocking collectives, shards(): square_tile = lax.all_gather(square_slab, 'layer', axis=0, tiled=True)  98.7 us
  transfers between devices with their start and end apart: 5, of which 5 were waited for; matrix products, arithmetic and copies ran while one was open for 0% of the time, Pallas kernels for 0%

commit v1 on v0

v1 whole, which is shorter than its diff:
```python
import jax
import jax.numpy as jnp
from jax import lax
from jax.experimental import pallas as pl
from jax.experimental.pallas import tpu as pltpu
from jax.sharding import PartitionSpec as P

MESH = pl.DeviceIdType.MESH
BS = 128
NC = 3
F32 = jnp.float32
BF16 = jnp.bfloat16


def kernel(density, occupancy, out, tile, left, right1, right2, part1, got1, square, square_got, part2, got2,
           final, final_got, slab_mask, out_mask,
           a1_s, a1_r, a2_s, a2_r, seed_s, seed_r, ring_s, ring_r, sib_s, sib_r,
           r1_s, r1_r, sq_s, sq_r, r2_s, r2_r, f_s, f_r):
    row, col, layer = (lax.axis_index(name) for name in ("row", "col", "layer"))
    group, zi = row // 4, row % 4
    y, core = col // 2, col % 2
    zh, x = layer // 4, layer % 4
    place = 4 * zh + group
    kind = (x + zi) % 4
    rights = (right1, right2)

    def device(x_=x, y_=y, core_=core, place_=place, zi_=zi):
        return {"row": 4 * (place_ % 4) + zi_, "col": 2 * y_ + core_, "layer": 4 * (place_ // 4) + x_}

    sibling = device(core_=1 - core)
    up, down = device(place_=(place + 1) % 8), device(place_=(place + 7) % 8)

    barrier = pltpu.get_barrier_semaphore()
    friends = [sibling, up, down]
    for step in range(1, 4):
        friends.append(device(y_=(y + step) % 4))
        for other in range(2):
            friends.append(device(zi_=(zi + step) % 4, core_=other))
            friends.append(device(x_=(x + step) % 4, core_=other))
    for friend in friends:
        pl.semaphore_signal(barrier, inc=1, device_id=friend, device_id_type=MESH)

    pattern = occupancy[...].astype(F32).astype(BF16)
    blocks = pattern.shape[0]

    def mask(row0, rows, col0, cols):
        row_block = (row0 + lax.broadcasted_iota(jnp.int32, (rows, blocks), 0)) // BS
        rows_hot = (row_block == lax.broadcasted_iota(jnp.int32, (rows, blocks), 1)).astype(F32).astype(BF16)
        col_block = (col0 + lax.broadcasted_iota(jnp.int32, (blocks, cols), 1)) // BS
        cols_hot = (col_block == lax.broadcasted_iota(jnp.int32, (blocks, cols), 0)).astype(F32).astype(BF16)
        chosen = jnp.dot(rows_hot, pattern, preferred_element_type=F32).astype(BF16)
        return jnp.dot(chosen, cols_hot, preferred_element_type=F32)

    tile[...] = density[...] * mask(384 * row, 384, 768 * col, 768).astype(BF16)
    pl.semaphore_wait(barrier, len(friends))

    pending = []

    def send(src, dst, send_sem, recv_sem, target, here=None, only=None):
        copy = pltpu.make_async_remote_copy(
            src_ref=src, dst_ref=dst, send_sem=send_sem, recv_sem=recv_sem, device_id=target, device_id_type=MESH
        )
        if here is None:
            go = only
        else:
            go = jnp.logical_not(here) if only is None else jnp.logical_and(only, jnp.logical_not(here))

            @pl.when(here if only is None else jnp.logical_and(only, here))
            def _():
                pltpu.make_async_copy(src, dst, recv_sem).start()

        if go is None:
            copy.start()
        else:
            pl.when(go)(copy.start)
        pending.append((copy, go))

    def arrive(dst, recv_sem):
        pltpu.make_async_remote_copy(
            src_ref=dst, dst_ref=dst, send_sem=recv_sem, recv_sem=recv_sem, device_id=sibling, device_id_type=MESH
        ).wait_recv()

    seed_zi = (zi + 4 - x) % 4
    for c in range(NC):
        for other in range(2):
            send(
                tile.at[pl.ds(pl.multiple_of(192 * zh + 96 * other, 32), 96),
                        pl.ds(pl.multiple_of(384 * (seed_zi % 2) + BS * c, BS), BS)],
                right1.at[c, pl.ds(pl.multiple_of(192 * (2 * group + zh) + 96 * other, 32), 96)],
                seed_s.at[2 * c + other], seed_r.at[c], device(zi_=seed_zi, core_=other),
                here=jnp.logical_and(seed_zi == zi, core == other), only=core == seed_zi // 2,
            )
    for h in range(2):
        to_zi = (2 * core + h + 4 - x) % 4
        send(
            tile.at[pl.ds(pl.multiple_of(192 * zh, 64), 192), pl.ds(384 * h, 384)],
            left.at[y, pl.ds(pl.multiple_of(192 * (zi % 2), 64), 192)],
            a1_s.at[h], a1_r.at[zi % 2], device(zi_=to_zi, core_=zi // 2),
            here=jnp.logical_and(to_zi == zi, zi // 2 == core),
        )

    def rows_of(place_, core_):
        return pl.multiple_of(192 * (2 * (place_ % 4) + place_ // 4) + 96 * core_, 32)

    def ring_piece(way, hop, core_):
        at = rows_of((place + (8 - hop if way == 0 else hop)) % 8, core_)
        if hop < 4:
            return pl.ds(at, 96)
        return pl.ds(pl.multiple_of(at + 48 * way, 16), 48)

    def ring_send(q, c, way, hop):
        rows = ring_piece(way, hop - 1, core)
        if hop == 4:
            rows = pl.ds(pl.multiple_of(rows.start + 48 * way, 16), 48)
        ref = rights[q].at[c, rows]
        n = ((q * NC + c) * 2 + way) * 4 + hop - 1
        send(ref, ref, ring_s.at[n], ring_r.at[n], up if way == 0 else down)

    def share(q, c, way, hop):
        ref = rights[q].at[c, ring_piece(way, hop, core)]
        n = (q * NC + c) * 9 + (0 if hop == 0 else 1 + 4 * way + hop - 1)
        send(ref, ref, sib_s.at[n], sib_r.at[n], sibling)

    def ring_open(q, c):
        ring_send(q, c, 0, 1)
        ring_send(q, c, 1, 1)
        share(q, c, 0, 0)

    def ring_hop(q, c, hop):
        for way in range(2):
            n = ((q * NC + c) * 2 + way) * 4 + hop - 1
            arrive(rights[q].at[c, ring_piece(way, hop, core)], ring_r.at[n])
            if hop < 4:
                ring_send(q, c, way, hop + 1)
            share(q, c, way, hop)

    def ring_close(q, c):
        for way, hop in [(0, 0)] + [(way, hop) for hop in range(1, 5) for way in range(2)]:
            n = (q * NC + c) * 9 + (0 if hop == 0 else 1 + 4 * way + hop - 1)
            arrive(rights[q].at[c, ring_piece(way, hop, 1 - core)], sib_r.at[n])

    def product(q, c):
        total = jnp.dot(left[0], rights[q][c, pl.ds(0, 384)], preferred_element_type=F32)
        for j in range(1, 4):
            total += jnp.dot(left[j], rights[q][c, pl.ds(384 * j, 384)], preferred_element_type=F32)
        return total

    own_rows = rows_of(place, core)

    for c in range(NC):
        arrive(right1.at[c, pl.ds(own_rows, 96)], seed_r.at[c])
        ring_open(0, c)
    for h in range(2):
        arrive(left.at[y, pl.ds(192 * h, 192)], a1_r.at[h])
    for step in range(1, 4):
        send(left.at[y], left.at[y], a2_s.at[step - 1], a2_r.at[step - 1], device(y_=(y + step) % 4))

    slab_mask[...] = mask(384 * (4 * group + kind) + 192 * zh + 96 * core, 96, 1536 * y + 384 * zi, 384)
    for h in range(2):
        out_mask[h] = mask(384 * (4 * group + 2 * core + h) + 192 * zh + 48 * x, 48, 1536 * y + 384 * zi, 384)

    for hop in range(1, 5):
        for c in range(NC):
            ring_hop(0, c, hop)
    for step in range(1, 4):
        arrive(left.at[(y + 4 - step) % 4], a2_r.at[step - 1])

    for c in range(NC):
        ring_close(0, c)
        part1[c] = product(0, c)
        for h in range(2):
            to_x = (2 * core + h + 4 - zi) % 4
            for other in range(2):
                send(
                    part1.at[c, pl.ds(192 * h + 96 * other, 96)], got1.at[c, x],
                    r1_s.at[4 * c + 2 * h + other], r1_r.at[4 * c + x], device(x_=to_x, core_=other),
                    here=jnp.logical_and(to_x == x, core == other),
                )
    for c in range(NC):
        for other in range(4):
            arrive(got1.at[c, other], r1_r.at[4 * c + other])
        total = (got1[c, 0] + got1[c, 1]) + (got1[c, 2] + got1[c, 3])
        rounded = (total * slab_mask[:, BS * c:BS * (c + 1)]).astype(BF16)
        right2[c, pl.ds(own_rows, 96)] = rounded
        square[:, BS * c:BS * (c + 1)] = rounded
        ring_open(1, c)
    for h in range(2):
        send(
            square.at[pl.ds(48 * h, 48)], square_got.at[kind % 2], sq_s.at[h], sq_r.at[kind % 2],
            device(x_=2 * core + h, core_=kind // 2),
            here=jnp.logical_and(2 * core + h == x, kind // 2 == core),
        )
    for hop in range(1, 5):
        for c in range(NC):
            ring_hop(1, c, hop)

    for c in range(NC):
        ring_close(1, c)
        total = product(1, c)
        for h in range(2):
            for k in range(4):
                part2[c, k, h] = total[192 * h + 48 * k:192 * h + 48 * (k + 1)]
        for step in range(1, 4):
            to_x = (x + step) % 4
            send(part2.at[c, to_x], got2.at[c, step - 1], r2_s.at[3 * c + step - 1], r2_r.at[3 * c + step - 1],
                 device(x_=to_x))
    for h in range(2):
        arrive(square_got.at[h], sq_r.at[h])
    for c in range(NC):
        for step in range(1, 4):
            arrive(got2.at[c, step - 1], r2_r.at[3 * c + step - 1])
        for h in range(2):
            total = (part2[c, x, h] + got2[c, 0, h]) + (got2[c, 1, h] + got2[c, 2, h])
            cube = total * out_mask[h, :, BS * c:BS * (c + 1)]
            final[c, h] = 3.0 * square_got[h, :, BS * c:BS * (c + 1)].astype(F32) - 2.0 * cube
            send(
                final.at[c, h], final_got.at[c, zi % 2], f_s.at[2 * c + h], f_r.at[2 * c + zi % 2],
                device(zi_=2 * core + h, core_=zi // 2),
                here=jnp.logical_and(2 * core + h == zi, zi // 2 == core),
            )
    for c in range(NC):
        for e in range(2):
            arrive(final_got.at[c, e], f_r.at[2 * c + e])
            out[:, 384 * e + BS * c:384 * e + BS * (c + 1)] = final_got[c, e]
    for copy, go in pending:
        if go is None:
            copy.wait_send()
        else:
            pl.when(go)(copy.wait_send)


def shards(density, occupancy):
    dma = pltpu.SemaphoreType.DMA
    return pl.pallas_call(
        kernel,
        name="purify",
        out_shape=jax.ShapeDtypeStruct((48, 768), F32),
        in_specs=[pl.BlockSpec(memory_space=pltpu.VMEM)] * 2,
        out_specs=pl.BlockSpec(memory_space=pltpu.VMEM),
        scratch_shapes=[
            pltpu.VMEM((384, 768), BF16),
            pltpu.VMEM((4, 384, 384), BF16),
            pltpu.VMEM((NC, 1536, BS), BF16),
            pltpu.VMEM((NC, 1536, BS), BF16),
            pltpu.VMEM((NC, 384, BS), F32),
            pltpu.VMEM((NC, 4, 96, BS), F32),
            pltpu.VMEM((96, 384), BF16),
            pltpu.VMEM((2, 48, 384), BF16),
            pltpu.VMEM((NC, 4, 2, 48, BS), F32),
            pltpu.VMEM((NC, 3, 2, 48, BS), F32),
            pltpu.VMEM((NC, 2, 48, BS), F32),
            pltpu.VMEM((NC, 2, 48, BS), F32),
            pltpu.VMEM((96, 384), F32),
            pltpu.VMEM((2, 48, 384), F32),
            dma((2,)), dma((2,)), dma((3,)), dma((3,)), dma((2 * NC,)), dma((NC,)),
            dma((16 * NC,)), dma((16 * NC,)), dma((18 * NC,)), dma((18 * NC,)),
            dma((4 * NC,)), dma((4 * NC,)), dma((2,)), dma((2,)),
            dma((3 * NC,)), dma((3 * NC,)), dma((2 * NC,)), dma((2 * NC,)),
        ],
        compiler_params=pltpu.CompilerParams(
            collective_id=0, has_side_effects=True, vmem_limit_bytes=32 * 1024 * 1024
        ),
        cost_estimate=pl.CostEstimate(flops=2 * 2 * 384 * 384 * 1536, bytes_accessed=2 * 384 * 768 + 4 * 48 * 768,
                                      transcendentals=0),
    )(density, occupancy)


def solution(mesh):
    return jax.shard_map(
        shards,
        mesh=mesh,
        in_specs=(P("row", "col"), P()),
        out_specs=P(("row", "layer"), "col"),
        check_vma=False,
    )
```

time: 1390 us -> 116 us (0.08)
  waiting for transfers between devices: 1260 us -> 0 us
  Pallas kernels: 0 us -> 112 us
  blocking collectives: 98.7 us -> 0 us
    psum x3 -> x0, waiting for transfers between devices: 827 us -> none  [from_root(): return lax.psum(kept, axis)]
    reduce_scatter x2 -> x0, waiting for transfers between devices: 436 us -> none  [reduce_rows(): lax.psum_scatter(partial_value, 'layer', scatter_dimension=0, tiled=True)]
    pallas_call x0 -> x1, Pallas kernels: none -> 112 us  [shards(): pl.pallas_call(kernel, name='purify', out_shape=jax.ShapeDtypeStruct((48,...]
    all_gather x1 -> x0, blocking collectives: 98.7 us -> none  [shards(): square_tile = lax.all_gather(square_slab, 'layer', axis=0, tiled=True)]
  transfers between devices with their start and end apart: 5 -> 0, of which waited for: 5 -> 0; matrix products, arithmetic and copies ran while one was open for 0% -> 0% of each run, Pallas kernels for 0% -> 0%
where the time goes in v1:
time: 116 us; the launch traced here: 114 us
  Pallas kernels  112 us (97%)
  local copies, waits for them, and re-layouts  2.46 us (2%)
    pallas_call x1, Pallas kernels, shards(): pl.pallas_call(kernel, name='purify', out_shape=jax.ShapeDtypeStruct((48,...  112 us
    unnamed x5, local copies, waits for them, and re-layouts  2.46 us

profile of v1, /device:TPU:1, one launch (start us, length us, event | category | flops | bytes accessed | tf_op | source)
XLA Modules:
  0.0 114.4 jit_solution(12109232667548235080)
XLA Ops:
  0.0 0.0 copy-start
  0.0 1.1 copy-done
  1.1 0.0 copy-start.1
  1.1 0.7 copy-done.1
  1.8 111.9 %purify.1 = f32[48,768]{1,0:T(8,128)S(1)} custom-call(bf16[384,768]{1,0:T(8,128)(2,1)S(1)} %copy-done, s32[48,48]{1,0:T(8,128)S(1)} %copy-done.1), custom_call_target="tpu_custom_call" | custom-call | flops 905969664 | bytes 737280 | tf_op jit(solution)/shard_map/purify/pallas_call | solution.py:234
  113.7 0.7 copy.4
Async XLA Ops:
  0.0 1.1 copy-start
  1.1 0.7 copy-start.1

commit v2 on v1

--- a/solution.py
+++ b/solution.py
@@ -81,44 +81,70 @@
         ).wait_recv()
 
     seed_zi = (zi + 4 - x) % 4
-    for c in range(NC):
+
+    def seeds(c):
         for other in range(2):
             send(
-                tile.at[pl.ds(pl.multiple_of(192 * zh + 96 * other, 32), 96),
-                        pl.ds(pl.multiple_of(384 * (seed_zi % 2) + BS * c, BS), BS)],
-                right1.at[c, pl.ds(pl.multiple_of(192 * (2 * group + zh) + 96 * other, 32), 96)],
+                tile.at[pl.ds(192 * other, 192), pl.ds(pl.multiple_of(384 * (seed_zi % 2) + BS * c, BS), BS)],
+                right1.at[c, pl.ds(pl.multiple_of(384 * group + 192 * other, 64), 192)],
                 seed_s.at[2 * c + other], seed_r.at[c], device(zi_=seed_zi, core_=other),
                 here=jnp.logical_and(seed_zi == zi, core == other), only=core == seed_zi // 2,
             )
-    for h in range(2):
-        to_zi = (2 * core + h + 4 - x) % 4
-        send(
-            tile.at[pl.ds(pl.multiple_of(192 * zh, 64), 192), pl.ds(384 * h, 384)],
-            left.at[y, pl.ds(pl.multiple_of(192 * (zi % 2), 64), 192)],
-            a1_s.at[h], a1_r.at[zi % 2], device(zi_=to_zi, core_=zi // 2),
-            here=jnp.logical_and(to_zi == zi, zi // 2 == core),
-        )
-
-    def rows_of(place_, core_):
-        return pl.multiple_of(192 * (2 * (place_ % 4) + place_ // 4) + 96 * core_, 32)
-
-    def ring_piece(way, hop, core_):
-        at = rows_of((place + (8 - hop if way == 0 else hop)) % 8, core_)
-        if hop < 4:
-            return pl.ds(at, 96)
-        return pl.ds(pl.multiple_of(at + 48 * way, 16), 48)
+
+    def left_group():
+        for h in range(2):
+            to_zi = (2 * core + h + 4 - x) % 4
+            send(
+                tile.at[pl.ds(pl.multiple_of(192 * zh, 64), 192), pl.ds(384 * h, 384)],
+                left.at[y, pl.ds(pl.multiple_of(192 * (zi % 2), 64), 192)],
+                a1_s.at[h], a1_r.at[zi % 2], device(zi_=to_zi, core_=zi // 2),
+                here=jnp.logical_and(to_zi == zi, zi // 2 == core),
+            )
+
+    def left_open():
+        for h in range(2):
+            arrive(left.at[y, pl.ds(192 * h, 192)], a1_r.at[h])
+        for way in range(2):
+            send(left.at[y], left.at[y], a2_s.at[way], a2_r.at[way], device(y_=(y + (3 if way else 1)) % 4))
+
+    def left_hop():
+        for way in range(2):
+            came = (y + (1 if way else 3)) % 4
+            arrive(left.at[came], a2_r.at[way])
+            ref = left.at[came, pl.ds(192 * way, 192)]
+            send(ref, ref, a2_s.at[2 + way], a2_r.at[2 + way], device(y_=(y + (3 if way else 1)) % 4))
+
+    def left_close():
+        for way in range(2):
+            arrive(left.at[(y + 2) % 4, pl.ds(192 * way, 192)], a2_r.at[2 + way])
+
+    hops = (2, 4)
+
+    def span(q, way, hop, core_, narrow):
+        away = (place + (8 - hop if way == 0 else hop)) % 8
+        if q == 0:
+            start, size = 384 * (away % 4) + 192 * core_, 192
+        else:
+            start, size = 384 * (away % 4) + 192 * (away // 4) + 96 * core_, 96
+        if narrow:
+            size //= 2
+            start = start + size * way
+        return pl.ds(pl.multiple_of(start, 16), size)
+
+    def ring_number(q, c, way, hop):
+        return 4 * NC * q + (2 * c + way) * hops[q] + hop - 1
+
+    def share_number(q, c, way, hop):
+        return 5 * NC * q + (2 * hops[q] + 1) * c + (0 if hop == 0 else 1 + way * hops[q] + hop - 1)
 
     def ring_send(q, c, way, hop):
-        rows = ring_piece(way, hop - 1, core)
-        if hop == 4:
-            rows = pl.ds(pl.multiple_of(rows.start + 48 * way, 16), 48)
-        ref = rights[q].at[c, rows]
-        n = ((q * NC + c) * 2 + way) * 4 + hop - 1
-        send(ref, ref, ring_s.at[n], ring_r.at[n], up if way == 0 else down)
+        ref = rights[q].at[c, span(q, way, hop - 1, core, hop == hops[q])]
+        n = ring_number(q, c, way, hop)
+        send(ref, ref, ring_s.at[n], ring_r.at[n], down if way else up)
 
     def share(q, c, way, hop):
-        ref = rights[q].at[c, ring_piece(way, hop, core)]
-        n = (q * NC + c) * 9 + (0 if hop == 0 else 1 + 4 * way + hop - 1)
+        ref = rights[q].at[c, span(q, way, hop, core, hop == hops[q])]
+        n = share_number(q, c, way, hop)
         send(ref, ref, sib_s.at[n], sib_r.at[n], sibling)
 
     def ring_open(q, c):
@@ -128,16 +154,19 @@
 
     def ring_hop(q, c, hop):
         for way in range(2):
-            n = ((q * NC + c) * 2 + way) * 4 + hop - 1
-            arrive(rights[q].at[c, ring_piece(way, hop, core)], ring_r.at[n])
-            if hop < 4:
+            arrive(rights[q].at[c, span(q, way, hop, core, hop == hops[q])], ring_r.at[ring_number(q, c, way, hop)])
+            if hop < hops[q]:
                 ring_send(q, c, way, hop + 1)
             share(q, c, way, hop)
 
     def ring_close(q, c):
-        for way, hop in [(0, 0)] + [(way, hop) for hop in range(1, 5) for way in range(2)]:
-            n = (q * NC + c) * 9 + (0 if hop == 0 else 1 + 4 * way + hop - 1)
-            arrive(rights[q].at[c, ring_piece(way, hop, 1 - core)], sib_r.at[n])
+        for hop in range(hops[q] + 1):
+            for way in range(2 if hop else 1):
+                arrive(rights[q].at[c, span(q, way, hop, 1 - core, hop == hops[q])], sib_r.at[share_number(q, c, way, hop)])
+
+    def seed_open(c):
+        arrive(right1.at[c, span(0, 0, 0, core, False)], seed_r.at[c])
+        ring_open(0, c)
 
     def product(q, c):
         total = jnp.dot(left[0], rights[q][c, pl.ds(0, 384)], preferred_element_type=F32)
@@ -145,27 +174,12 @@
             total += jnp.dot(left[j], rights[q][c, pl.ds(384 * j, 384)], preferred_element_type=F32)
         return total
 
-    own_rows = rows_of(place, core)
-
-    for c in range(NC):
-        arrive(right1.at[c, pl.ds(own_rows, 96)], seed_r.at[c])
-        ring_open(0, c)
-    for h in range(2):
-        arrive(left.at[y, pl.ds(192 * h, 192)], a1_r.at[h])
-    for step in range(1, 4):
-        send(left.at[y], left.at[y], a2_s.at[step - 1], a2_r.at[step - 1], device(y_=(y + step) % 4))
-
-    slab_mask[...] = mask(384 * (4 * group + kind) + 192 * zh + 96 * core, 96, 1536 * y + 384 * zi, 384)
-    for h in range(2):
-        out_mask[h] = mask(384 * (4 * group + 2 * core + h) + 192 * zh + 48 * x, 48, 1536 * y + 384 * zi, 384)
-
-    for hop in range(1, 5):
-        for c in range(NC):
-            ring_hop(0, c, hop)
-    for step in range(1, 4):
-        arrive(left.at[(y + 4 - step) % 4], a2_r.at[step - 1])
-
-    for c in range(NC):
+    def masks():
+        slab_mask[...] = mask(384 * (4 * group + kind) + 192 * zh + 96 * core, 96, 1536 * y + 384 * zi, 384)
+        for h in range(2):
+            out_mask[h] = mask(384 * (4 * group + 2 * core + h) + 192 * zh + 48 * x, 48, 1536 * y + 384 * zi, 384)
+
+    def square_part(c):
         ring_close(0, c)
         part1[c] = product(0, c)
         for h in range(2):
@@ -176,25 +190,25 @@
                     r1_s.at[4 * c + 2 * h + other], r1_r.at[4 * c + x], device(x_=to_x, core_=other),
                     here=jnp.logical_and(to_x == x, core == other),
                 )
-    for c in range(NC):
+
+    def square_sum(c):
         for other in range(4):
             arrive(got1.at[c, other], r1_r.at[4 * c + other])
         total = (got1[c, 0] + got1[c, 1]) + (got1[c, 2] + got1[c, 3])
         rounded = (total * slab_mask[:, BS * c:BS * (c + 1)]).astype(BF16)
-        right2[c, pl.ds(own_rows, 96)] = rounded
+        right2[c, span(1, 0, 0, core, False)] = rounded
         square[:, BS * c:BS * (c + 1)] = rounded
         ring_open(1, c)
-    for h in range(2):
-        send(
-            square.at[pl.ds(48 * h, 48)], square_got.at[kind % 2], sq_s.at[h], sq_r.at[kind % 2],
-            device(x_=2 * core + h, core_=kind // 2),
-            here=jnp.logical_and(2 * core + h == x, kind // 2 == core),
-        )
-    for hop in range(1, 5):
-        for c in range(NC):
-            ring_hop(1, c, hop)
-
-    for c in range(NC):
+
+    def square_rows():
+        for h in range(2):
+            send(
+                square.at[pl.ds(48 * h, 48)], square_got.at[kind % 2], sq_s.at[h], sq_r.at[kind % 2],
+                device(x_=2 * core + h, core_=kind // 2),
+                here=jnp.logical_and(2 * core + h == x, kind // 2 == core),
+            )
+
+    def cube_part(c):
         ring_close(1, c)
         total = product(1, c)
         for h in range(2):
@@ -204,9 +218,8 @@
             to_x = (x + step) % 4
             send(part2.at[c, to_x], got2.at[c, step - 1], r2_s.at[3 * c + step - 1], r2_r.at[3 * c + step - 1],
                  device(x_=to_x))
-    for h in range(2):
-        arrive(square_got.at[h], sq_r.at[h])
-    for c in range(NC):
+
+    def cube_sum(c):
         for step in range(1, 4):
             arrive(got2.at[c, step - 1], r2_r.at[3 * c + step - 1])
         for h in range(2):
@@ -218,10 +231,58 @@
                 device(zi_=2 * core + h, core_=zi // 2),
                 here=jnp.logical_and(2 * core + h == zi, zi // 2 == core),
             )
-    for c in range(NC):
+
+    def finish(c):
         for e in range(2):
             arrive(final_got.at[c, e], f_r.at[2 * c + e])
             out[:, 384 * e + BS * c:384 * e + BS * (c + 1)] = final_got[c, e]
+
+    seeds(0)
+    left_group()
+    seeds(1)
+    seeds(2)
+    seed_open(0)
+    left_open()
+    seed_open(1)
+    masks()
+    ring_hop(0, 0, 1)
+    seed_open(2)
+    left_hop()
+    ring_hop(0, 0, 2)
+    ring_hop(0, 1, 1)
+    left_close()
+    square_part(0)
+    ring_hop(0, 1, 2)
+    ring_hop(0, 2, 1)
+    square_part(1)
+    square_sum(0)
+    ring_hop(0, 2, 2)
+    square_part(2)
+    square_sum(1)
+    ring_hop(1, 0, 1)
+    square_sum(2)
+    square_rows()
+    ring_hop(1, 1, 1)
+    ring_hop(1, 0, 2)
+    ring_hop(1, 2, 1)
+    ring_hop(1, 1, 2)
+    ring_hop(1, 0, 3)
+    ring_hop(1, 2, 2)
+    ring_hop(1, 1, 3)
+    ring_hop(1, 0, 4)
+    ring_hop(1, 2, 3)
+    ring_hop(1, 1, 4)
+    cube_part(0)
+    ring_hop(1, 2, 4)
+    cube_part(1)
+    for h in range(2):
+        arrive(square_got.at[h], sq_r.at[h])
+    cube_part(2)
+    cube_sum(0)
+    cube_sum(1)
+    cube_sum(2)
+    for c in range(NC):
+        finish(c)
     for copy, go in pending:
         if go is None:
             copy.wait_send()
@@ -252,8 +313,8 @@
             pltpu.VMEM((NC, 2, 48, BS), F32),
             pltpu.VMEM((96, 384), F32),
             pltpu.VMEM((2, 48, 384), F32),
-            dma((2,)), dma((2,)), dma((3,)), dma((3,)), dma((2 * NC,)), dma((NC,)),
-            dma((16 * NC,)), dma((16 * NC,)), dma((18 * NC,)), dma((18 * NC,)),
+            dma((2,)), dma((2,)), dma((4,)), dma((4,)), dma((2 * NC,)), dma((NC,)),
+            dma((12 * NC,)), dma((12 * NC,)), dma((14 * NC,)), dma((14 * NC,)),
             dma((4 * NC,)), dma((4 * NC,)), dma((2,)), dma((2,)),
             dma((3 * NC,)), dma((3 * NC,)), dma((2 * NC,)), dma((2 * NC,)),
         ],

time: 116 us -> 113 us (0.974)
  Pallas kernels: 112 us -> 110 us
    pallas_call x1, Pallas kernels: 112 us -> 110 us  [shards(): pl.pallas_call(kernel, name='purify', out_shape=jax.ShapeDtypeStruct((48,...]
where the time goes in v2:
time: 113 us; the launch traced here: 112 us
  Pallas kernels  110 us (97%)
  local copies, waits for them, and re-layouts  2.46 us (2%)
    pallas_call x1, Pallas kernels, shards(): pl.pallas_call(kernel, name='purify', out_shape=jax.ShapeDtypeStruct((48,...  110 us
    unnamed x5, local copies, waits for them, and re-layouts  2.46 us

profile of v2, /device:TPU:1, one launch (start us, length us, event | category | flops | bytes accessed | tf_op | source)
XLA Modules:
  0.0 112.3 jit_solution(16870685445966368836)
XLA Ops:
  0.0 0.0 copy-start
  0.0 1.1 copy-done
  1.1 0.0 copy-start.1
  1.1 0.7 copy-done.1
  1.8 109.8 %purify.1 = f32[48,768]{1,0:T(8,128)S(1)} custom-call(bf16[384,768]{1,0:T(8,128)(2,1)S(1)} %copy-done, s32[48,48]{1,0:T(8,128)S(1)} %copy-done.1), custom_call_target="tpu_custom_call" | custom-call | flops 905969664 | bytes 737280 | tf_op jit(solution)/shard_map/purify/pallas_call | solution.py:295
  111.6 0.7 copy.4
Async XLA Ops:
  0.0 1.1 copy-start
  1.1 0.7 copy-start.1

commit v3 on v2

v3 whole, which is shorter than its diff:
```python
import jax
import jax.numpy as jnp
from jax import lax
from jax.experimental import pallas as pl
from jax.experimental.pallas import tpu as pltpu
from jax.sharding import PartitionSpec as P

MESH = pl.DeviceIdType.MESH
BS = 128
NC = 3
NP = 4
ROWS = 384 // NP
F32 = jnp.float32
BF16 = jnp.bfloat16


def kernel(density, occupancy, out, tile, left, right1, right2, part1, got1, square, part2, got2, final, final_got,
           slab_mask, a1_s, a1_r, a2_s, a2_r, a3_s, a3_r, seed_s, seed_r, ring_s, ring_r,
           r1_s, r1_r, sq_s, sq_r, r2_s, r2_r, f_s, f_r):
    row, col, layer = (lax.axis_index(name) for name in ("row", "col", "layer"))
    y, core = col // 2, col % 2
    zh, x = layer // 4, layer % 4
    z = 16 * zh + row
    pair, zi = z // 2, z % 2
    low = pair % 8
    kind = (x + zi) % 4
    is_root = kind // 2 == pair % 2
    not_root = jnp.logical_not(is_root)
    rights = (right1, right2)

    def device(x_=x, y_=y, core_=core, z_=z):
        return {"row": z_ % 16, "col": 2 * y_ + core_, "layer": 4 * (z_ // 16) + x_}

    def mate(zi_, core_):
        return device(z_=2 * pair + zi_, core_=core_)

    sibling = device(core_=1 - core)
    ahead = (device(z_=(z + 2) % 32), device(z_=(z + 30) % 32))
    beside = (device(y_=(y + 1) % 4), device(y_=(y + 3) % 4))

    barrier = pltpu.get_barrier_semaphore()
    friends = [sibling, mate(1 - zi, 0), mate(1 - zi, 1), *ahead, *beside]
    friends += [device(x_=(x + step) % 4) for step in range(1, 4)]
    for friend in friends:
        pl.semaphore_signal(barrier, inc=1, device_id=friend, device_id_type=MESH)

    pattern = occupancy[...].astype(F32).astype(BF16)
    blocks = pattern.shape[0]

    def mask(row0, rows, col0, cols):
        row_block = (row0 + lax.broadcasted_iota(jnp.int32, (rows, blocks), 0)) // BS
        rows_hot = (row_block == lax.broadcasted_iota(jnp.int32, (rows, blocks), 1)).astype(F32).astype(BF16)
        col_block = (col0 + lax.broadcasted_iota(jnp.int32, (blocks, cols), 1)) // BS
        cols_hot = (col_block == lax.broadcasted_iota(jnp.int32, (blocks, cols), 0)).astype(F32).astype(BF16)
        chosen = jnp.dot(rows_hot, pattern, preferred_element_type=F32).astype(BF16)
        return jnp.dot(chosen, cols_hot, preferred_element_type=F32)

    tile[...] = density[...] * mask(384 * row, 384, 768 * col, 768).astype(BF16)
    pl.semaphore_wait(barrier, len(friends))

    pending = []

    def send(src, dst, send_sem, recv_sem, target, here=None, only=None):
        copy = pltpu.make_async_remote_copy(
            src_ref=src, dst_ref=dst, send_sem=send_sem, recv_sem=recv_sem, device_id=target, device_id_type=MESH
        )
        if here is None:
            go = only
        else:
            go = jnp.logical_not(here) if only is None else jnp.logical_and(only, jnp.logical_not(here))

            @pl.when(here if only is None else jnp.logical_and(only, here))
            def _():
                pltpu.make_async_copy(src, dst, recv_sem).start()

        if go is None:
            copy.start()
        else:
            pl.when(go)(copy.start)
        pending.append((copy, go))

    def arrive(dst, recv_sem):
        pltpu.make_async_remote_copy(
            src_ref=dst, dst_ref=dst, send_sem=recv_sem, recv_sem=recv_sem, device_id=sibling, device_id_type=MESH
        ).wait_recv()

    seed_zi = (row + 4 - x % 4) % 4

    def seeds(c):
        for other in range(2):
            send(
                tile.at[:, pl.ds(384 * other + BS * c, BS)],
                right1.at[c, pl.ds(pl.multiple_of(384 * (low // 2), 128), 384)],
                seed_s.at[2 * c + other], seed_r.at[c], mate(seed_zi % 2, other),
                here=jnp.logical_and(seed_zi == zi, core == other),
                only=jnp.logical_and(seed_zi < 2, core == seed_zi),
            )

    def left_rows(j, core_, start=0, size=384):
        return left.at[j, pl.ds(pl.multiple_of(384 * core_ + start, 64), size)]

    def left_group():
        for to_zi in range(2):
            to_kind = (x + to_zi) % 4
            send(
                tile.at[:, pl.ds(pl.multiple_of(384 * (to_kind % 2), BS), 384)], left_rows(y, zi),
                a1_s.at[to_zi], a1_r.at[0], mate(to_zi, zi),
                here=jnp.logical_and(zi == to_zi, core == zi), only=core == to_kind // 2,
            )

    def left_share(j, n, start=0, size=384):
        ref = left_rows(j, core, start, size)
        send(ref, ref, a3_s.at[n], a3_r.at[n], sibling)

    def left_open():
        ref = left_rows(y, core)
        arrive(ref, a1_r.at[0])
        for way in range(2):
            send(ref, ref, a2_s.at[way], a2_r.at[way], beside[way])
        left_share(y, 0)

    def left_hop():
        for way in range(2):
            came = (y + (1 if way else 3)) % 4
            arrive(left_rows(came, core), a2_r.at[way])
            ref = left_rows(came, core, 192 * way, 192)
            send(ref, ref, a2_s.at[2 + way], a2_r.at[2 + way], beside[way])
            left_share(came, 1 + way)

    def left_last():
        for way in range(2):
            arrive(left_rows((y + 2) % 4, core, 192 * way, 192), a2_r.at[2 + way])
            left_share((y + 2) % 4, 3 + way, 192 * way, 192)

    def left_close():
        arrive(left_rows(y, 1 - core), a3_r.at[0])
        for way in range(2):
            arrive(left_rows((y + (1 if way else 3)) % 4, 1 - core), a3_r.at[1 + way])
            arrive(left_rows((y + 2) % 4, 1 - core, 192 * way, 192), a3_r.at[3 + way])

    def ring_rows(way, stage, piece):
        far = jnp.where(is_root, 2 * stage, 2 * stage - 1)
        from_pair = (pair + (far if way else 16 - far)) % 16
        return pl.ds(pl.multiple_of(384 * ((from_pair % 8) // 2) + ROWS * piece, 32), ROWS)

    def ring_number(q, c, way, stage, piece):
        return (((q * NC + c) * 2 + way) * 2 + stage - 1) * NP + piece

    def is_half(way, piece):
        return piece * 2 // NP == way

    def own_rows(piece=0, size=384):
        return pl.ds(pl.multiple_of(384 * (low // 2) + ROWS * piece, 32), size)

    def ring_open(q, c):
        for piece in range(NP):
            for way in range(2):
                ref = rights[q].at[c, own_rows(piece, ROWS)]
                send(ref, ref, ring_s.at[(((q * NC + c) * 2 + way) * 3) * NP + piece],
                     ring_r.at[ring_number(q, c, way, 1, piece)], ahead[way], only=is_root)

    def ring_first(q, c):
        for piece in range(NP):
            for way in range(2):
                n = ring_number(q, c, way, 1, piece)
                ref = rights[q].at[c, ring_rows(way, 1, piece)]
                arrive(ref, ring_r.at[n])
                send(ref, ref, ring_s.at[(((q * NC + c) * 2 + way) * 3 + 1) * NP + piece],
                     ring_r.at[n + jnp.where(is_root, NP, 0)], ahead[way])

    def ring_second(q, c):
        for piece in range(NP):
            for way in range(2):
                n = ring_number(q, c, way, 2, piece)
                ref = rights[q].at[c, ring_rows(way, 2, piece)]
                if is_half(way, piece):
                    arrive(ref, ring_r.at[n])
                    send(ref, ref, ring_s.at[(((q * NC + c) * 2 + way) * 3 + 2) * NP + piece], ring_r.at[n],
                         ahead[way], only=not_root)
                else:
                    pl.when(not_root)(lambda ref=ref, n=n: arrive(ref, ring_r.at[n]))

    def seed_open(c):
        pl.when(is_root)(lambda: arrive(right1.at[c, own_rows()], seed_r.at[c]))
        ring_open(0, c)

    def masks():
        for a in range(2):
            for h in range(2):
                slab_mask[a, h] = mask(384 * (2 * low + a) + 192 * h + 48 * x, 48, 1536 * y + 768 * zi + 384 * core, 384)

    def square_part(c):
        total = jnp.dot(left[0], right1[c, pl.ds(0, 384)], preferred_element_type=F32)
        for j in range(1, 4):
            total += jnp.dot(left[j], right1[c, pl.ds(384 * j, 384)], preferred_element_type=F32)
        for a in range(2):
            for h in range(2):
                for k in range(4):
                    part1[c, k, a, h] = total[384 * a + 192 * h + 48 * k:384 * a + 192 * h + 48 * (k + 1)]
        for step in range(1, 4):
            to_x = (x + step) % 4
            send(part1.at[c, to_x], got1.at[c, step - 1], r1_s.at[3 * c + step - 1], r1_r.at[3 * c + step - 1],
                 device(x_=to_x))

    def square_sum(c):
        for step in range(1, 4):
            arrive(got1.at[c, step - 1], r1_r.at[3 * c + step - 1])
        for a in range(2):
            to_x = (2 * low + a + 4 - zi) % 4
            for h in range(2):
                total = (part1[c, x, a, h] + got1[c, 0, a, h]) + (got1[c, 1, a, h] + got1[c, 2, a, h])
                square[c, a, h] = (total * slab_mask[a, h, :, BS * c:BS * (c + 1)]).astype(BF16)
                send(
                    square.at[c, a, h],
                    right2.at[c, pl.ds(pl.multiple_of(384 * (low // 2) + 192 * h + 48 * x, 16), 48)],
                    sq_s.at[4 * c + 2 * a + h], sq_r.at[8 * c + 2 * x + h], device(x_=to_x), here=to_x == x,
                )

    def square_open(c):
        def slabs():
            for k in range(4):
                for h in range(2):
                    arrive(right2.at[c, pl.ds(pl.multiple_of(384 * (low // 2) + 192 * h + 48 * k, 16), 48)],
                           sq_r.at[8 * c + 2 * k + h])

        pl.when(is_root)(slabs)
        ring_open(1, c)

    def cube_part(c):
        for a in range(2):
            rows = pl.ds(pl.multiple_of(384 * a + 192 * zh, 64), 192)
            total = jnp.dot(left[0, rows], right2[c, pl.ds(0, 384)], preferred_element_type=F32)
            for j in range(1, 4):
                total += jnp.dot(left[j, rows], right2[c, pl.ds(384 * j, 384)], preferred_element_type=F32)
            for k in range(4):
                part2[c, k, a] = total[48 * k:48 * (k + 1)]
        for step in range(1, 4):
            to_x = (x + step) % 4
            send(part2.at[c, to_x], got2.at[c, step - 1], r2_s.at[3 * c + step - 1], r2_r.at[3 * c + step - 1],
                 device(x_=to_x))

    def cube_sum(c):
        for step in range(1, 4):
            arrive(got2.at[c, step - 1], r2_r.at[3 * c + step - 1])
        for a in range(2):
            total = (part2[c, x, a] + got2[c, 0, a]) + (got2[c, 1, a] + got2[c, 2, a])
            cube = total * slab_mask[a, zh, :, BS * c:BS * (c + 1)]
            final[c, a] = 3.0 * square[c, a, zh].astype(F32) - 2.0 * cube
            send(
                final.at[c, a], final_got.at[c, core], f_s.at[2 * c + a], f_r.at[2 * c + core], mate(a, zi),
                here=jnp.logical_and(zi == a, core == zi),
            )

    def finish(c):
        for e in range(2):
            arrive(final_got.at[c, e], f_r.at[2 * c + e])
            out[:, 384 * e + BS * c:384 * e + BS * (c + 1)] = final_got[c, e]

    seeds(0)
    left_group()
    seeds(1)
    seeds(2)
    seed_open(0)
    left_open()
    seed_open(1)
    ring_first(0, 0)
    seed_open(2)
    masks()
    left_hop()
    ring_first(0, 1)
    ring_second(0, 0)
    left_last()
    left_close()
    square_part(0)
    ring_first(0, 2)
    ring_second(0, 1)
    square_part(1)
    square_sum(0)
    ring_second(0, 2)
    square_part(2)
    square_sum(1)
    square_open(0)
    square_sum(2)
    square_open(1)
    ring_first(1, 0)
    square_open(2)
    ring_first(1, 1)
    ring_second(1, 0)
    cube_part(0)
    ring_first(1, 2)
    ring_second(1, 1)
    cube_part(1)
    cube_sum(0)
    ring_second(1, 2)
    cube_part(2)
    cube_sum(1)
    cube_sum(2)
    for c in range(NC):
        finish(c)
    for copy, go in pending:
        if go is None:
            copy.wait_send()
        else:
            pl.when(go)(copy.wait_send)


def shards(density, occupancy):
    dma = pltpu.SemaphoreType.DMA
    return pl.pallas_call(
        kernel,
        name="purify",
        out_shape=jax.ShapeDtypeStruct((48, 768), F32),
        in_specs=[pl.BlockSpec(memory_space=pltpu.VMEM)] * 2,
        out_specs=pl.BlockSpec(memory_space=pltpu.VMEM),
        scratch_shapes=[
            pltpu.VMEM((384, 768), BF16),
            pltpu.VMEM((4, 768, 384), BF16),
            pltpu.VMEM((NC, 1536, BS), BF16),
            pltpu.VMEM((NC, 1536, BS), BF16),
            pltpu.VMEM((NC, 4, 2, 2, 48, BS), F32),
            pltpu.VMEM((NC, 3, 2, 2, 48, BS), F32),
            pltpu.VMEM((NC, 2, 2, 48, BS), BF16),
            pltpu.VMEM((NC, 4, 2, 48, BS), F32),
            pltpu.VMEM((NC, 3, 2, 48, BS), F32),
            pltpu.VMEM((NC, 2, 48, BS), F32),
            pltpu.VMEM((NC, 2, 48, BS), F32),
            pltpu.VMEM((2, 2, 48, 384), F32),
            dma((2,)), dma((1,)), dma((4,)), dma((4,)), dma((5,)), dma((5,)), dma((2 * NC,)), dma((NC,)),
            dma((12 * NC * NP,)), dma((8 * NC * NP,)),
            dma((3 * NC,)), dma((3 * NC,)), dma((4 * NC,)), dma((8 * NC,)),
            dma((3 * NC,)), dma((3 * NC,)), dma((2 * NC,)), dma((2 * NC,)),
        ],
        compiler_params=pltpu.CompilerParams(
            collective_id=0, has_side_effects=True, vmem_limit_bytes=32 * 1024 * 1024
        ),
        cost_estimate=pl.CostEstimate(flops=3 * 2 * 384 * 384 * 1536, bytes_accessed=2 * 384 * 768 + 4 * 48 * 768,
                                      transcendentals=0),
    )(density, occupancy)


def solution(mesh):
    return jax.shard_map(
        shards,
        mesh=mesh,
        in_specs=(P("row", "col"), P()),
        out_specs=P(("row", "layer"), "col"),
        check_vma=False,
    )
```

time: 113 us -> 116 us (1.027)
  Pallas kernels: 110 us -> 114 us
    pallas_call x1, Pallas kernels: 110 us -> 114 us  [shards(): pl.pallas_call(kernel, name='purify', out_shape=jax.ShapeDtypeStruct((48,...]
where the time goes in v3:
time: 116 us
  Pallas kernels  114 us (98%)
  local copies, waits for them, and re-layouts  2.46 us (2%)
    pallas_call x1, Pallas kernels, shards(): pl.pallas_call(kernel, name='purify', out_shape=jax.ShapeDtypeStruct((48,...  114 us
    unnamed x5, local copies, waits for them, and re-layouts  2.46 us

profile of v3, /device:TPU:1, one launch (start us, length us, event | category | flops | bytes accessed | tf_op | source)
XLA Modules:
  0.0 116.1 jit_solution(5829947648120675106)
XLA Ops:
  0.0 0.0 copy-start
  0.0 1.1 copy-done
  1.1 0.0 copy-start.1
  1.1 0.7 copy-done.1
  1.8 113.6 %purify.1 = f32[48,768]{1,0:T(8,128)S(1)} custom-call(bf16[384,768]{1,0:T(8,128)(2,1)S(1)} %copy-done, s32[48,48]{1,0:T(8,128)S(1)} %copy-done.1), custom_call_target="tpu_custom_call" | custom-call | flops 1358954496 | bytes 737280 | tf_op jit(solution)/shard_map/purify/pallas_call | solution.py:309
  115.4 0.7 copy.4
Async XLA Ops:
  0.0 1.1 copy-start
  1.1 0.7 copy-start.1

commit v4 on v2

--- a/solution.py
+++ b/solution.py
@@ -12,7 +12,7 @@
 BF16 = jnp.bfloat16
 
 
-def kernel(density, occupancy, out, tile, left, right1, right2, part1, got1, square, square_got, part2, got2,
+def kernel(density, occupancy, out, raw, raw_sem, tile, left, right1, right2, part1, got1, square, square_got, part2, got2,
            final, final_got, slab_mask, out_mask,
            a1_s, a1_r, a2_s, a2_r, seed_s, seed_r, ring_s, ring_r, sib_s, sib_r,
            r1_s, r1_r, sq_s, sq_r, r2_s, r2_r, f_s, f_r):
@@ -27,9 +27,19 @@
     def device(x_=x, y_=y, core_=core, place_=place, zi_=zi):
         return {"row": 4 * (place_ % 4) + zi_, "col": 2 * y_ + core_, "layer": 4 * (place_ // 4) + x_}
 
+    twist = jnp.where(zi % 2 == 1, 2, -2)
+    away = jnp.where(x == 0, 0, jnp.where(x == 1, -1, jnp.where(x == 2, twist, 1)))
+    seed_to, seed_from = 4 * place + zi + away + 32, 4 * place + zi - away + 32
+    lag = seed_from // 4 - place
+
+    def chip(z_, core_):
+        return device(core_=core_, place_=(z_ // 4) % 8, zi_=z_ % 4)
+
     sibling = device(core_=1 - core)
     up, down = device(place_=(place + 1) % 8), device(place_=(place + 7) % 8)
 
+    load = pltpu.make_async_copy(density, raw, raw_sem.at[0])
+    load.start()
     barrier = pltpu.get_barrier_semaphore()
     friends = [sibling, up, down]
     for step in range(1, 4):
@@ -40,6 +50,12 @@
     for friend in friends:
         pl.semaphore_signal(barrier, inc=1, device_id=friend, device_id_type=MESH)
 
+    @pl.when(x != 0)
+    def _():
+        for other in range(2):
+            pl.semaphore_signal(barrier, inc=1, device_id=chip(seed_to, other), device_id_type=MESH)
+            pl.semaphore_signal(barrier, inc=1, device_id=chip(seed_from, other), device_id_type=MESH)
+
     pattern = occupancy[...].astype(F32).astype(BF16)
     blocks = pattern.shape[0]
 
@@ -51,8 +67,10 @@
         chosen = jnp.dot(rows_hot, pattern, preferred_element_type=F32).astype(BF16)
         return jnp.dot(chosen, cols_hot, preferred_element_type=F32)
 
-    tile[...] = density[...] * mask(384 * row, 384, 768 * col, 768).astype(BF16)
-    pl.semaphore_wait(barrier, len(friends))
+    occupied = mask(384 * row, 384, 768 * col, 768).astype(BF16)
+    load.wait()
+    tile[...] = raw[...] * occupied
+    pl.semaphore_wait(barrier, len(friends) + jnp.where(x == 0, 0, 4))
 
     pending = []
 
@@ -80,15 +98,15 @@
             src_ref=dst, dst_ref=dst, send_sem=recv_sem, recv_sem=recv_sem, device_id=sibling, device_id_type=MESH
         ).wait_recv()
 
-    seed_zi = (zi + 4 - x) % 4
+    seed_zi = seed_to % 4
 
     def seeds(c):
         for other in range(2):
             send(
                 tile.at[pl.ds(192 * other, 192), pl.ds(pl.multiple_of(384 * (seed_zi % 2) + BS * c, BS), BS)],
                 right1.at[c, pl.ds(pl.multiple_of(384 * group + 192 * other, 64), 192)],
-                seed_s.at[2 * c + other], seed_r.at[c], device(zi_=seed_zi, core_=other),
-                here=jnp.logical_and(seed_zi == zi, core == other), only=core == seed_zi // 2,
+                seed_s.at[2 * c + other], seed_r.at[c], chip(seed_to, other),
+                here=jnp.logical_and(x == 0, core == other), only=core == seed_zi // 2,
             )
 
     def left_group():
@@ -121,11 +139,11 @@
     hops = (2, 4)
 
     def span(q, way, hop, core_, narrow):
-        away = (place + (8 - hop if way == 0 else hop)) % 8
+        at = (place + (8 - hop if way == 0 else hop)) % 8
         if q == 0:
-            start, size = 384 * (away % 4) + 192 * core_, 192
+            start, size = 384 * ((at + lag) % 4) + 192 * core_, 192
         else:
-            start, size = 384 * (away % 4) + 192 * (away // 4) + 96 * core_, 96
+            start, size = 384 * (at % 4) + 192 * (at // 4) + 96 * core_, 96
         if narrow:
             size //= 2
             start = start + size * way
@@ -180,7 +198,6 @@
             out_mask[h] = mask(384 * (4 * group + 2 * core + h) + 192 * zh + 48 * x, 48, 1536 * y + 384 * zi, 384)
 
     def square_part(c):
-        ring_close(0, c)
         part1[c] = product(0, c)
         for h in range(2):
             to_x = (2 * core + h + 4 - zi) % 4
@@ -198,7 +215,6 @@
         rounded = (total * slab_mask[:, BS * c:BS * (c + 1)]).astype(BF16)
         right2[c, span(1, 0, 0, core, False)] = rounded
         square[:, BS * c:BS * (c + 1)] = rounded
-        ring_open(1, c)
 
     def square_rows():
         for h in range(2):
@@ -209,7 +225,6 @@
             )
 
     def cube_part(c):
-        ring_close(1, c)
         total = product(1, c)
         for h in range(2):
             for k in range(4):
@@ -237,52 +252,62 @@
             arrive(final_got.at[c, e], f_r.at[2 * c + e])
             out[:, 384 * e + BS * c:384 * e + BS * (c + 1)] = final_got[c, e]
 
+    left_group()
     seeds(0)
-    left_group()
     seeds(1)
-    seeds(2)
     seed_open(0)
     left_open()
+    masks()
     seed_open(1)
-    masks()
     ring_hop(0, 0, 1)
+    seeds(2)
+    left_hop()
     seed_open(2)
-    left_hop()
     ring_hop(0, 0, 2)
     ring_hop(0, 1, 1)
     left_close()
+    ring_close(0, 0)
     square_part(0)
+    ring_hop(0, 2, 1)
     ring_hop(0, 1, 2)
-    ring_hop(0, 2, 1)
+    square_sum(0)
+    ring_close(0, 1)
+    ring_open(1, 0)
     square_part(1)
-    square_sum(0)
     ring_hop(0, 2, 2)
+    ring_close(0, 2)
     square_part(2)
+    ring_hop(1, 0, 1)
     square_sum(1)
-    ring_hop(1, 0, 1)
+    ring_open(1, 1)
     square_sum(2)
+    ring_open(1, 2)
     square_rows()
+    ring_hop(1, 0, 2)
     ring_hop(1, 1, 1)
-    ring_hop(1, 0, 2)
     ring_hop(1, 2, 1)
+    ring_hop(1, 0, 3)
     ring_hop(1, 1, 2)
-    ring_hop(1, 0, 3)
     ring_hop(1, 2, 2)
     ring_hop(1, 1, 3)
+    ring_hop(1, 2, 3)
     ring_hop(1, 0, 4)
-    ring_hop(1, 2, 3)
+    ring_close(1, 0)
+    cube_part(0)
     ring_hop(1, 1, 4)
-    cube_part(0)
+    ring_close(1, 1)
     ring_hop(1, 2, 4)
     cube_part(1)
+    ring_close(1, 2)
+    cube_part(2)
     for h in range(2):
         arrive(square_got.at[h], sq_r.at[h])
-    cube_part(2)
     cube_sum(0)
     cube_sum(1)
     cube_sum(2)
-    for c in range(NC):
-        finish(c)
+    finish(1)
+    finish(0)
+    finish(2)
     for copy, go in pending:
         if go is None:
             copy.wait_send()
@@ -296,9 +321,11 @@
         kernel,
         name="purify",
         out_shape=jax.ShapeDtypeStruct((48, 768), F32),
-        in_specs=[pl.BlockSpec(memory_space=pltpu.VMEM)] * 2,
+        in_specs=[pl.BlockSpec(memory_space=pltpu.HBM), pl.BlockSpec(memory_space=pltpu.VMEM)],
         out_specs=pl.BlockSpec(memory_space=pltpu.VMEM),
         scratch_shapes=[
+            pltpu.VMEM((384, 768), BF16),
+            dma((1,)),
             pltpu.VMEM((384, 768), BF16),
             pltpu.VMEM((4, 384, 384), BF16),
             pltpu.VMEM((NC, 1536, BS), BF16),
@@ -319,7 +346,7 @@
             dma((3 * NC,)), dma((3 * NC,)), dma((2 * NC,)), dma((2 * NC,)),
         ],
         compiler_params=pltpu.CompilerParams(
-            collective_id=0, has_side_effects=True, vmem_limit_bytes=32 * 1024 * 1024
+            collective_id=0, has_side_effects=True, vmem_limit_bytes=60 * 1024 * 1024
         ),
         cost_estimate=pl.CostEstimate(flops=2 * 2 * 384 * 384 * 1536, bytes_accessed=2 * 384 * 768 + 4 * 48 * 768,
                                       transcendentals=0),

time: 113 us -> 114 us (level)
  Pallas kernels: 110 us -> 112 us
    pallas_call x1, Pallas kernels: 110 us -> 112 us  [shards(): pl.pallas_call(kernel, name='purify', out_shape=jax.ShapeDtypeStruct((48,...]
    unnamed x5 -> x1, local copies, waits for them, and re-layouts: 2.46 us -> 1.58 us
where the time goes in v4:
time: 114 us
  Pallas kernels  112 us (98%)
  local copies, waits for them, and re-layouts  1.58 us (1%)
    pallas_call x1, Pallas kernels, shards(): pl.pallas_call(kernel, name='purify', out_shape=jax.ShapeDtypeStruct((48,...  112 us

profile of v4, /device:TPU:1, one launch (start us, length us, event | category | flops | bytes accessed | tf_op | source)
XLA Modules:
  0.0 113.6 jit_solution(1473302333635671557)
XLA Ops:
  0.0 112.1 %purify.1 = f32[48,768]{1,0:T(8,128)} custom-call(bf16[384,768]{1,0:T(8,128)(2,1)} %density.1, s32[48,48]{1,0:T(8,128)} %occupancy.1), custom_call_target="tpu_custom_call" | custom-call | flops 905969664 | bytes 737280 | tf_op jit(solution)/shard_map/purify/pallas_call | solution.py:320
  112.1 1.6 %copy.4 = f32[48,768]{1,0:T(8,128)} copy(f32[48,768]{1,0:T(8,128)} %purify.1) | data formatting | bytes 294912

commit v5 on v4

--- a/solution.py
+++ b/solution.py
@@ -13,7 +13,7 @@
 
 
 def kernel(density, occupancy, out, raw, raw_sem, tile, left, right1, right2, part1, got1, square, square_got, part2, got2,
-           final, final_got, slab_mask, out_mask,
+           final, final_got, slab_mask, out_mask, early,
            a1_s, a1_r, a2_s, a2_r, seed_s, seed_r, ring_s, ring_r, sib_s, sib_r,
            r1_s, r1_r, sq_s, sq_r, r2_s, r2_r, f_s, f_r):
     row, col, layer = (lax.axis_index(name) for name in ("row", "col", "layer"))
@@ -93,6 +93,14 @@
             pl.when(go)(copy.start)
         pending.append((copy, go))
 
+    def settle(most):
+        for copy, go in pending[:most]:
+            if go is None:
+                copy.wait_send()
+            else:
+                pl.when(go)(copy.wait_send)
+        del pending[:most]
+
     def arrive(dst, recv_sem):
         pltpu.make_async_remote_copy(
             src_ref=dst, dst_ref=dst, send_sem=recv_sem, recv_sem=recv_sem, device_id=sibling, device_id_type=MESH
@@ -177,8 +185,8 @@
                 ring_send(q, c, way, hop + 1)
             share(q, c, way, hop)
 
-    def ring_close(q, c):
-        for hop in range(hops[q] + 1):
+    def ring_close(q, c, first=0, last=None):
+        for hop in range(first, (hops[q] if last is None else last) + 1):
             for way in range(2 if hop else 1):
                 arrive(rights[q].at[c, span(q, way, hop, 1 - core, hop == hops[q])], sib_r.at[share_number(q, c, way, hop)])
 
@@ -224,8 +232,20 @@
                 here=jnp.logical_and(2 * core + h == x, kind // 2 == core),
             )
 
+    def cube_early(c):
+        ring_close(1, c, 0, 3)
+        total = None
+        for step in range(1, 4):
+            j = (group + step) % 4
+            rows = right2[c, pl.ds(pl.multiple_of(384 * j, 128), 384)]
+            term = jnp.dot(left[j], rows, preferred_element_type=F32)
+            total = term if total is None else total + term
+        early[c] = total
+
     def cube_part(c):
-        total = product(1, c)
+        ring_close(1, c, 4)
+        rows = right2[c, pl.ds(pl.multiple_of(384 * group, 128), 384)]
+        total = early[c] + jnp.dot(left[group], rows, preferred_element_type=F32)
         for h in range(2):
             for k in range(4):
                 part2[c, k, h] = total[192 * h + 48 * k:192 * h + 48 * (k + 1)]
@@ -283,36 +303,38 @@
     square_sum(2)
     ring_open(1, 2)
     square_rows()
+    settle(20)
     ring_hop(1, 0, 2)
     ring_hop(1, 1, 1)
     ring_hop(1, 2, 1)
+    settle(20)
     ring_hop(1, 0, 3)
     ring_hop(1, 1, 2)
     ring_hop(1, 2, 2)
+    settle(20)
     ring_hop(1, 1, 3)
+    cube_early(0)
     ring_hop(1, 2, 3)
     ring_hop(1, 0, 4)
-    ring_close(1, 0)
+    cube_early(1)
+    ring_hop(1, 1, 4)
     cube_part(0)
-    ring_hop(1, 1, 4)
-    ring_close(1, 1)
+    cube_early(2)
     ring_hop(1, 2, 4)
     cube_part(1)
-    ring_close(1, 2)
+    settle(20)
     cube_part(2)
     for h in range(2):
         arrive(square_got.at[h], sq_r.at[h])
     cube_sum(0)
     cube_sum(1)
+    settle(20)
     cube_sum(2)
+    settle(len(pending) - 6)
+    finish(0)
     finish(1)
-    finish(0)
     finish(2)
-    for copy, go in pending:
-        if go is None:
-            copy.wait_send()
-        else:
-            pl.when(go)(copy.wait_send)
+    settle(len(pending))
 
 
 def shards(density, occupancy):
@@ -340,6 +362,7 @@
             pltpu.VMEM((NC, 2, 48, BS), F32),
             pltpu.VMEM((96, 384), F32),
             pltpu.VMEM((2, 48, 384), F32),
+            pltpu.VMEM((NC, 384, BS), F32),
             dma((2,)), dma((2,)), dma((4,)), dma((4,)), dma((2 * NC,)), dma((NC,)),
             dma((12 * NC,)), dma((12 * NC,)), dma((14 * NC,)), dma((14 * NC,)),
             dma((4 * NC,)), dma((4 * NC,)), dma((2,)), dma((2,)),

time: 114 us -> 114 us (level)
  no operation moved by 1% of the time
where the time goes in v5:
time: 114 us
  Pallas kernels  112 us (98%)
  local copies, waits for them, and re-layouts  1.58 us (1%)
    pallas_call x1, Pallas kernels, shards(): pl.pallas_call(kernel, name='purify', out_shape=jax.ShapeDtypeStruct((48,...  112 us

profile of v5, /device:TPU:1, one launch (start us, length us, event | category | flops | bytes accessed | tf_op | source)
XLA Modules:
  0.0 113.8 jit_solution(3620189028523631259)
XLA Ops:
  0.0 112.2 %purify.1 = f32[48,768]{1,0:T(8,128)} custom-call(bf16[384,768]{1,0:T(8,128)(2,1)} %density.1, s32[48,48]{1,0:T(8,128)} %occupancy.1), custom_call_target="tpu_custom_call" | custom-call | flops 905969664 | bytes 737280 | tf_op jit(solution)/shard_map/purify/pallas_call | solution.py:342
  112.2 1.6 %copy.4 = f32[48,768]{1,0:T(8,128)} copy(f32[48,768]{1,0:T(8,128)} %purify.1) | data formatting | bytes 294912

commit v6 on v2

--- a/solution.py
+++ b/solution.py
@@ -13,7 +13,7 @@
 
 
 def kernel(density, occupancy, out, tile, left, right1, right2, part1, got1, square, square_got, part2, got2,
-           final, final_got, slab_mask, out_mask,
+           final, final_got, slab_mask, out_mask, early,
            a1_s, a1_r, a2_s, a2_r, seed_s, seed_r, ring_s, ring_r, sib_s, sib_r,
            r1_s, r1_r, sq_s, sq_r, r2_s, r2_r, f_s, f_r):
     row, col, layer = (lax.axis_index(name) for name in ("row", "col", "layer"))
@@ -74,6 +74,14 @@
         else:
             pl.when(go)(copy.start)
         pending.append((copy, go))
+
+    def settle(most):
+        for copy, go in pending[:most]:
+            if go is None:
+                copy.wait_send()
+            else:
+                pl.when(go)(copy.wait_send)
+        del pending[:most]
 
     def arrive(dst, recv_sem):
         pltpu.make_async_remote_copy(
@@ -159,8 +167,8 @@
                 ring_send(q, c, way, hop + 1)
             share(q, c, way, hop)
 
-    def ring_close(q, c):
-        for hop in range(hops[q] + 1):
+    def ring_close(q, c, first=0, last=None):
+        for hop in range(first, (hops[q] if last is None else last) + 1):
             for way in range(2 if hop else 1):
                 arrive(rights[q].at[c, span(q, way, hop, 1 - core, hop == hops[q])], sib_r.at[share_number(q, c, way, hop)])
 
@@ -208,9 +216,20 @@
                 here=jnp.logical_and(2 * core + h == x, kind // 2 == core),
             )
 
+    def cube_early(c):
+        ring_close(1, c, 0, 3)
+        total = None
+        for step in range(1, 4):
+            j = (group + step) % 4
+            rows = right2[c, pl.ds(pl.multiple_of(384 * j, 128), 384)]
+            term = jnp.dot(left[j], rows, preferred_element_type=F32)
+            total = term if total is None else total + term
+        early[c] = total
+
     def cube_part(c):
-        ring_close(1, c)
-        total = product(1, c)
+        ring_close(1, c, 4)
+        rows = right2[c, pl.ds(pl.multiple_of(384 * group, 128), 384)]
+        total = early[c] + jnp.dot(left[group], rows, preferred_element_type=F32)
         for h in range(2):
             for k in range(4):
                 part2[c, k, h] = total[192 * h + 48 * k:192 * h + 48 * (k + 1)]
@@ -262,32 +281,36 @@
     ring_hop(1, 0, 1)
     square_sum(2)
     square_rows()
+    settle(16)
     ring_hop(1, 1, 1)
     ring_hop(1, 0, 2)
     ring_hop(1, 2, 1)
+    settle(16)
     ring_hop(1, 1, 2)
     ring_hop(1, 0, 3)
     ring_hop(1, 2, 2)
+    settle(16)
     ring_hop(1, 1, 3)
+    cube_early(0)
     ring_hop(1, 0, 4)
     ring_hop(1, 2, 3)
+    cube_early(1)
     ring_hop(1, 1, 4)
     cube_part(0)
+    settle(16)
+    cube_early(2)
     ring_hop(1, 2, 4)
     cube_part(1)
+    cube_part(2)
     for h in range(2):
         arrive(square_got.at[h], sq_r.at[h])
-    cube_part(2)
     cube_sum(0)
     cube_sum(1)
     cube_sum(2)
+    settle(len(pending) - 6)
     for c in range(NC):
         finish(c)
-    for copy, go in pending:
-        if go is None:
-            copy.wait_send()
-        else:
-            pl.when(go)(copy.wait_send)
+    settle(len(pending))
 
 
 def shards(density, occupancy):
@@ -313,6 +336,7 @@
             pltpu.VMEM((NC, 2, 48, BS), F32),
             pltpu.VMEM((96, 384), F32),
             pltpu.VMEM((2, 48, 384), F32),
+            pltpu.VMEM((NC, 384, BS), F32),
             dma((2,)), dma((2,)), dma((4,)), dma((4,)), dma((2 * NC,)), dma((NC,)),
             dma((12 * NC,)), dma((12 * NC,)), dma((14 * NC,)), dma((14 * NC,)),
             dma((4 * NC,)), dma((4 * NC,)), dma((2,)), dma((2,)),

time: 113 us -> 112 us (level)
  no operation moved by 1% of the time
where the time goes in v6:
time: 112 us
  Pallas kernels  109 us (97%)
  local copies, waits for them, and re-layouts  2.46 us (2%)
    pallas_call x1, Pallas kernels, shards(): pl.pallas_call(kernel, name='purify', out_shape=jax.ShapeDtypeStruct((48,...  109 us
    unnamed x5, local copies, waits for them, and re-layouts  2.46 us

profile of v6, /device:TPU:1, one launch (start us, length us, event | category | flops | bytes accessed | tf_op | source)
XLA Modules:
  0.0 111.9 jit_solution(7770827611972375495)
XLA Ops:
  0.0 0.0 copy-start
  0.0 1.1 copy-done
  1.1 0.0 copy-start.1
  1.1 0.7 copy-done.1
  1.8 109.5 %purify.1 = f32[48,768]{1,0:T(8,128)S(1)} custom-call(bf16[384,768]{1,0:T(8,128)(2,1)S(1)} %copy-done, s32[48,48]{1,0:T(8,128)S(1)} %copy-done.1), custom_call_target="tpu_custom_call" | custom-call | flops 905969664 | bytes 737280 | tf_op jit(solution)/shard_map/purify/pallas_call | solution.py:318
  111.3 0.7 copy.4
Async XLA Ops:
  0.0 1.1 copy-start
  1.1 0.7 copy-start.1

commit v7 on v5

--- a/solution.py
+++ b/solution.py
@@ -272,68 +272,66 @@
             arrive(final_got.at[c, e], f_r.at[2 * c + e])
             out[:, 384 * e + BS * c:384 * e + BS * (c + 1)] = final_got[c, e]
 
+    seeds(0)
     left_group()
-    seeds(0)
     seeds(1)
+    seeds(2)
     seed_open(0)
     left_open()
+    seed_open(1)
     masks()
-    seed_open(1)
     ring_hop(0, 0, 1)
-    seeds(2)
+    seed_open(2)
     left_hop()
-    seed_open(2)
     ring_hop(0, 0, 2)
     ring_hop(0, 1, 1)
     left_close()
     ring_close(0, 0)
     square_part(0)
+    ring_hop(0, 1, 2)
     ring_hop(0, 2, 1)
-    ring_hop(0, 1, 2)
+    ring_close(0, 1)
+    square_part(1)
     square_sum(0)
-    ring_close(0, 1)
     ring_open(1, 0)
-    square_part(1)
     ring_hop(0, 2, 2)
     ring_close(0, 2)
     square_part(2)
-    ring_hop(1, 0, 1)
     square_sum(1)
     ring_open(1, 1)
+    ring_hop(1, 0, 1)
     square_sum(2)
     ring_open(1, 2)
     square_rows()
-    settle(20)
+    settle(16)
+    ring_hop(1, 1, 1)
     ring_hop(1, 0, 2)
-    ring_hop(1, 1, 1)
     ring_hop(1, 2, 1)
-    settle(20)
+    settle(16)
+    ring_hop(1, 1, 2)
     ring_hop(1, 0, 3)
-    ring_hop(1, 1, 2)
     ring_hop(1, 2, 2)
-    settle(20)
+    settle(16)
     ring_hop(1, 1, 3)
     cube_early(0)
+    ring_hop(1, 0, 4)
     ring_hop(1, 2, 3)
-    ring_hop(1, 0, 4)
     cube_early(1)
     ring_hop(1, 1, 4)
     cube_part(0)
+    settle(16)
     cube_early(2)
     ring_hop(1, 2, 4)
     cube_part(1)
-    settle(20)
     cube_part(2)
     for h in range(2):
         arrive(square_got.at[h], sq_r.at[h])
     cube_sum(0)
     cube_sum(1)
-    settle(20)
     cube_sum(2)
     settle(len(pending) - 6)
-    finish(0)
-    finish(1)
-    finish(2)
+    for c in range(NC):
+        finish(c)
     settle(len(pending))
 
 

time: 114 us -> 113 us (level)
  the two profiles are of different devices: /device:TPU:1 before, /device:TPU:24 now
where the time goes in v7:
time: 113 us; the launch traced here: 112 us
  Pallas kernels  111 us (98%)
  local copies, waits for them, and re-layouts  1.58 us (1%)
    pallas_call x1, Pallas kernels, shards(): pl.pallas_call(kernel, name='purify', out_shape=jax.ShapeDtypeStruct((48,...  111 us

profile of v7, /device:TPU:24, one launch (start us, length us, event | category | flops | bytes accessed | tf_op | source)
XLA Modules:
  0.0 112.3 jit_solution(1165192015316049579)
XLA Ops:
  0.0 110.7 %purify.1 = f32[48,768]{1,0:T(8,128)} custom-call(bf16[384,768]{1,0:T(8,128)(2,1)} %density.1, s32[48,48]{1,0:T(8,128)} %occupancy.1), custom_call_target="tpu_custom_call" | custom-call | flops 905969664 | bytes 737280 | tf_op jit(solution)/shard_map/purify/pallas_call | solution.py:340
  110.7 1.6 %copy.4 = f32[48,768]{1,0:T(8,128)} copy(f32[48,768]{1,0:T(8,128)} %purify.1) | data formatting | bytes 294912
